TPU v7x, 32 devices: a whole 2x2x4 slice. The times are simulated.
32 devices in a mesh: grp: 2 (over y), role: 2 (over core), ctx: 8 (over z, x).
Axes of the slice: x: 2, y: 2, z: 4, core: 2. Of those that a mesh axis runs over, the one named last changes fastest.
Arguments:
- teacher_streams: bfloat16 [3, 8192, 4096], P(None, ('grp', 'ctx'), 'role'), parts along dimension 1, may hold values from -6 to 6
- conv_filter: bfloat16 [4096, 128], P('role'), may hold values from -0.5 to 0.5
- map_weight: bfloat16 [4096, 2048], P(('role', 'ctx')), may hold values from -0.125 to 0.125
- bases: int32 [8192], P(('grp', 'ctx')), parts along dimension 0, may hold values from 0 to 3
- base_weights: float32 [4], replicated, may hold values from 0.25 to 2
- student_qkv: bfloat16 [3, 8192, 2048], P(None, ('grp', 'ctx'), 'role'), parts along dimension 1, may hold values from -6 to 6
Outputs:
- student_grads: bfloat16 [3, 8192, 2048], P(None, ('grp', 'ctx'), 'role'), parts along dimension 1
There are 2 independent parts, one for each index of `grp`. A program takes and returns all parts, laid end to end along the dimension named above; an argument that names none is the same for every part. Nothing has to cross between parts.
All inputs are finite; a program needn't handle non-finite values.
Results may differ from a plain program's by a relative error of at most 0.0055.
Values may be sent and summed in bfloat16 or wider, within the bound.
A program may use at most 192 MiB of HBM per device.

v0:
```python
from functools import reduce
import jax
import jax.numpy as jnp
from jax import lax
from jax.sharding import PartitionSpec as P

DH = 128
BLK = 512


def from_behind(value, axis, steps):
    count = lax.axis_size(axis)
    leading, last = (max(0, -steps), min(count, count - steps))
    return lax.ppermute(value, axis, [(source, source + steps) for source in range(leading, last)])


def prefix(value, axis, join, neutral, backward):
    count, mine = (lax.axis_size(axis), lax.axis_index(axis))
    pieces = lax.all_gather(value, axis)
    if backward:
        pieces = pieces[::-1]
        mine = count - 1 - mine
    so_far = jnp.full_like(value, 0) + jnp.asarray(neutral, value.dtype)

    def turn(position, so_far):
        longer = join(so_far, pieces[position])
        return jnp.where(position < mine, longer, so_far)

    return lax.fori_loop(0, count - 1, turn, so_far)


def depthwise(extended, filters):
    kernel = jnp.flip(filters, axis=1).T[:, None, :]
    result = lax.conv_general_dilated(
        extended[None],
        kernel,
        (1,),
        "VALID",
        dimension_numbers=("NWC", "WIO", "NWC"),
        feature_group_count=extended.shape[1],
        preferred_element_type=jnp.float32,
    )
    return result[0]


def add_states(earlier, later):
    return earlier + later


def on_device(teacher_streams, conv_filter, map_weight, bases, base_weights, student_qkv):
    gate_in = teacher_streams[0]
    mixed_in = (
        teacher_streams[1].astype(jnp.float32) * teacher_streams[2].astype(jnp.float32)
    ).astype(jnp.bfloat16)
    tok_rows = mixed_in.shape[0]
    rim_rows = conv_filter.shape[1] - 1
    left_rim = from_behind(mixed_in[tok_rows - rim_rows :], "ctx", 1)
    conv_out = depthwise(jnp.concatenate([left_rim, mixed_in], 0), conv_filter)
    teacher_out = (gate_in.astype(jnp.float32) * conv_out).astype(jnp.bfloat16)
    zero_map = jnp.zeros((tok_rows, map_weight.shape[1]), jnp.float32)
    shard_rows = lax.all_gather(map_weight, "ctx", axis=0, tiled=True)
    columns = lax.slice_in_dim(teacher_out, 0, shard_rows.shape[0], axis=1)
    partial_map = zero_map + jnp.dot(columns, shard_rows, preferred_element_type=jnp.float32)
    target = lax.psum_scatter(partial_map, "role", scatter_dimension=1, tiled=True)
    head_width = student_qkv.shape[2]
    heads_dev = head_width // DH
    queries = student_qkv[0].reshape(tok_rows, heads_dev, DH)
    keys_all = student_qkv[1].reshape(tok_rows, heads_dev, DH)
    values_all = student_qkv[2].reshape(tok_rows, heads_dev, DH)
    att_scale = float(DH * tok_rows * lax.axis_size("ctx")) ** (-0.5)
    nblocks = tok_rows // BLK
    causal = (jnp.arange(BLK)[:, None] >= jnp.arange(BLK)[None, :])[None]
    state_terms = [
        jnp.einsum("shd,she->hde", keys_all, values_all, preferred_element_type=jnp.float32)
    ]
    zero_state = jnp.zeros((heads_dev, DH, DH), jnp.float32)
    own_state = reduce(jnp.add, state_terms)
    carried = prefix(own_state, "ctx", add_states, zero_state, False)
    outputs = []
    block = 0
    prefix_bf = carried.astype(jnp.bfloat16)
    scores = jnp.einsum("thd,shd->hts", queries, keys_all, preferred_element_type=jnp.float32)
    scores_bf = jnp.where(causal, scores, 0.0).astype(jnp.bfloat16)
    block_out = att_scale * (
        jnp.einsum("thd,hde->the", queries, prefix_bf, preferred_element_type=jnp.float32)
        + jnp.einsum("hts,she->the", scores_bf, values_all, preferred_element_type=jnp.float32)
    )
    prefixes = [prefix_bf]
    kept_scores = [scores_bf]
    outputs.append(block_out.reshape(BLK, head_width))
    outputs = outputs[0]
    onehot = (bases[:, None] == jnp.arange(base_weights.shape[0])[None, :]).astype(jnp.float32)
    tok_weight = jnp.sum(onehot * base_weights[None, :], axis=1)
    resid_bf = (
        (tok_weight[:, None] * (outputs - target))
        .astype(jnp.bfloat16)
        .reshape(tok_rows, heads_dev, DH)
    )
    back_terms = [jnp.einsum("thd,the->hde", queries, resid_bf, preferred_element_type=jnp.float32)]
    own_back = reduce(jnp.add, back_terms)
    later_sum = prefix(own_back, "ctx", add_states, zero_state, True)
    grad_blocks = [None] * nblocks
    for block in reversed(range(nblocks)):
        later_bf = later_sum.astype(jnp.bfloat16)
        later_sum = later_sum + back_terms[block]
        scores_bf = kept_scores[block]
        grad_scores = jnp.where(
            causal,
            jnp.einsum("the,she->hts", resid_bf, values_all, preferred_element_type=jnp.float32),
            0.0,
        ).astype(jnp.bfloat16)
        grad_query = att_scale * (
            jnp.einsum(
                "the,hde->thd", resid_bf, prefixes[block], preferred_element_type=jnp.float32
            )
            + jnp.einsum("hts,shd->thd", grad_scores, keys_all, preferred_element_type=jnp.float32)
        )
        grad_key = att_scale * (
            jnp.einsum("she,hde->shd", values_all, later_bf, preferred_element_type=jnp.float32)
            + jnp.einsum("hts,thd->shd", grad_scores, queries, preferred_element_type=jnp.float32)
        )
        grad_value = att_scale * (
            jnp.einsum("shd,hde->she", keys_all, later_bf, preferred_element_type=jnp.float32)
            + jnp.einsum("hts,the->she", scores_bf, resid_bf, preferred_element_type=jnp.float32)
        )
        grad_blocks[block] = jnp.stack(
            [
                grad_query.reshape(BLK, head_width),
                grad_key.reshape(BLK, head_width),
                grad_value.reshape(BLK, head_width),
            ],
            0,
        ).astype(jnp.bfloat16)
    return grad_blocks[0]


def solution(mesh):
    in_specs = (
        P(None, ("grp", "ctx"), "role"),
        P("role", None),
        P(("role", "ctx"), None),
        P(("grp", "ctx")),
        P(),
        P(None, ("grp", "ctx"), "role"),
    )
    out_specs = P(None, ("grp", "ctx"), "role")
    return jax.shard_map(
        on_device, mesh=mesh, in_specs=in_specs, out_specs=out_specs, check_vma=False
    )
```

profile of v0, /device:TPU:0, one launch (start us, length us, event | category | flops | bytes accessed | tf_op | source)
XLA Modules:
  0.0 349.2 jit_solution(2665267496531229638)
XLA Ops:
  6.5 0.7 all-gather.6.cloned.1.call-update
  7.3 0.0 all-gather.8.cloned.1.call-start
  7.3 3.2 multiply_convert_fusion
  10.5 1.0 slice_bitcast_fusion
  11.5 5.6 %collective-permute-start = (bf16[127,2048]{1,0:T(8,128)(2,1)}, bf16[127,2048]{1,0:T(8,128)(2,1)}, u32[]{:S(2)}, u32[]{:S(2)}) collective-permute-start(bf16[127,2048]{1,0:T(8,128)(2,1)} %slice_bitcast_fusion), channel_id=1, source_target_pairs={{0,1},{1,2},{2,3},{3,4},{4,5},{5,6},{6,7},{8,9},{9,10},{10,11},{11... | collective-permute-start | bytes 1560584 | tf_op jit(solution)/shard_map/ppermute | solution.py:14
  17.1 1.3 fusion.17
  18.4 0.5 copy.112
  19.0 0.5 copy.75
  19.5 1.2 fusion.18
  20.8 0.0 all-gather.8.cloned.1.call-update
  20.8 0.0 reduce-scatter.2.cloned.1.call-start
  20.9 0.2 copy-done.12
  21.0 1.5 rev.7
  22.5 0.9 copy.85
  23.4 3.0 fusion.42
  26.5 8.9 %collective-permute-done = bf16[127,2048]{1,0:T(8,128)(2,1)} collective-permute-done((bf16[127,2048]{1,0:T(8,128)(2,1)}, bf16[127,2048]{1,0:T(8,128)(2,1)}, u32[]{:S(2)}, u32[]{:S(2)}) %collective-permute-start) | collective-permute-done | bytes 520224 | tf_op jit(solution)/shard_map/ppermute | solution.py:14
  35.4 1.7 maximum_bitcast_fusion
  37.1 65.3 %fusion = bf16[1,512,2048]{2,0,1:T(2,128)(2,1)} fusion(bf16[128,1,2048]{2,1,0:T(2,128)(2,1)S(1)} %copy.85, bf16[1,639,2048]{2,1,0:T(8,128)(2,1)S(1)} %maximum_bitcast_fusion, bf16[1,512,2048]{2,1,0:T(8,128)(2,1)S(1)} %slice-done), kind=kOutput, calls=%fused_computation.5 | convolution fusion | flops 271581184 | bytes 7335936 | tf_op jit(solution)/shard_map/conv_general_dilated | solution.py:34
  102.4 40.9 %all-gather.6.cloned.1.call-done = bf16[2048,2048]{1,0:T(8,128)(2,1)} async-done(((bf16[256,2048]{1,0:T(8,128)(2,1)}), bf16[2048,2048]{1,0:T(8,128)(2,1)}) %all-gather.6.cloned.1.call-update) | async-done | bytes 8388624 | tf_op jit(solution)/shard_map/all_gather | solution.py:61
  143.2 11.5 %fusion.2 = f32[512,2048]{1,0:T(8,128)} fusion(bf16[2048,2048]{1,0:T(8,128)(2,1)} %all-gather.6.cloned.1.call-done, bf16[1,512,2048]{2,0,1:T(2,128)(2,1)} %fusion), kind=kOutput, calls=%fused_computation.11 | convolution fusion | flops 4294967296 | bytes 14680064 | tf_op jit(solution)/shard_map/dot_general | solution.py:63
  154.8 0.2 all-gather.10.cloned.1.call-start
  155.0 1.6 copy.113
  156.6 0.1 select_reduce_fusion
  156.7 0.1 iota_compare_fusion
  156.8 3.3 select_convert_fusion.1
  160.1 56.9 %all-gather.8.cloned.1.call-done = f32[64,128,128]{2,1,0:T(8,128)} async-done(((f32[8,128,128]{2,1,0:T(8,128)}), f32[64,128,128]{2,1,0:T(8,128)}) %all-gather.8.cloned.1.call-update) | async-done | bytes 4194320 | tf_op jit(solution)/shard_map/all_gather | solution.py:19
  217.0 8.8 %while.28 = (s32[]{:T(128)}, f32[8,128,128]{2,1,0:T(8,128)S(1)}, s32[]{:T(128)}, f32[8,8,128,128]{3,2,1,0:T(8,128)}, s32[]{:T(128)}, /*index=5*/s32[]{:T(128)}) while((s32[]{:T(128)}, f32[8,128,128]{2,1,0:T(8,128)S(1)}, s32[]{:T(128)}, f32[8,8,128,128]{3,2,1,0:T(8,128)}, s32[]{:T(128)}, /*index=5*/s32[]{:T(128)}) %tuple.75), condition=%wide.region_1.2_spmd.clone, body=%wide.region_0.1_spmd.clone.sunk | while | flops 393220 | bytes 1572965 | solution.py:29
  217.0 1.2 add_select_fusion.4
  218.2 1.2 add_select_fusion.4
  219.5 1.2 add_select_fusion.4
  220.7 1.2 add_select_fusion.4
  222.0 1.2 add_select_fusion.4
  223.2 1.3 add_select_fusion.4
  224.5 1.2 add_select_fusion.4
  225.8 0.5 fusion.15
  226.3 1.0 copy-done.1
  227.3 5.2 %fusion.9 = f32[512,8,128]{0,2,1:T(8,128)} fusion(f32[8,128,512]{2,1,0:T(8,128)S(1)} %fusion.15, bf16[8,512,512]{2,1,0:T(8,128)(2,1)} %select_convert_fusion.1, bf16[512,8,128]{0,2,1:T(8,128)(2,1)S(1)} %bitcast.79), kind=kOutput, calls=%fused_computation.21 | convolution fusion | flops 537919488 | bytes 9437184 | tf_op jit(solution)/shard_map/hts,she->the/dot_general | solution.py:86
  232.5 3.0 copy.86
  235.5 3.5 multiply_convert_fusion.2
  239.0 1.5 copy.114
  240.5 1.6 convolution_bitcast_fusion
  242.1 1.0 copy.92
  243.2 0.4 fusion.13
  243.6 1.4 select_convert_fusion
  245.0 2.5 fusion.8
  247.5 2.3 copy.97
  249.7 4.4 %fusion.19 = f32[8,128,512]{2,1,0:T(8,128)} fusion(bf16[512,8,128]{0,2,1:T(8,128)(2,1)S(1)} %bitcast.85, bf16[8,512,512]{2,1,0:T(8,128)(2,1)} %select_convert_fusion.1), kind=kOutput, calls=%fused_computation.38 | convolution fusion | flops 536870912 | bytes 7340032 | tf_op jit(solution)/shard_map/hts,the->she/dot_general | solution.py:124
  254.2 61.3 %all-gather.10.cloned.1.call-done = f32[64,128,128]{2,1,0:T(8,128)} async-done(((f32[8,128,128]{2,1,0:T(8,128)}), f32[64,128,128]{2,1,0:T(8,128)}) %all-gather.10.cloned.1.call-update) | async-done | bytes 4194320 | tf_op jit(solution)/shard_map/all_gather | solution.py:19
  315.5 4.6 %rev.8 = f32[8,8,128,128]{3,2,1,0:T(8,128)} reverse(f32[8,8,128,128]{3,2,1,0:T(8,128)} %bitcast.95), dimensions={0} | reverse | bytes 8388608 | tf_op jit(solution)/shard_map/rev | solution.py:21
  320.1 8.7 %while.29 = (s32[]{:T(128)}, f32[8,128,128]{2,1,0:T(8,128)S(1)}, s32[]{:T(128)}, f32[8,8,128,128]{3,2,1,0:T(8,128)}, s32[]{:T(128)}, /*index=5*/s32[]{:T(128)}) while((s32[]{:T(128)}, f32[8,128,128]{2,1,0:T(8,128)S(1)}, s32[]{:T(128)}, f32[8,8,128,128]{3,2,1,0:T(8,128)}, s32[]{:T(128)}, /*index=5*/s32[]{:T(128)}) %tuple.64), condition=%wide.region_5.6_spmd.clone, body=%wide.region_4.5_spmd.clone.sunk | while | flops 393220 | bytes 1572965 | solution.py:29
  320.1 1.2 add_select_fusion.5
  321.4 1.2 add_select_fusion.5
  322.6 1.2 add_select_fusion.5
  323.9 1.2 add_select_fusion.5
  325.1 1.2 add_select_fusion.5
  326.4 1.2 add_select_fusion.5
  327.6 1.2 add_select_fusion.5
  328.9 1.8 fusion.11
  330.6 0.9 copy-done.9
  331.5 1.5 multiply_convert_fusion.1
  333.0 1.5 copy.99
  334.5 4.7 %fusion.6 = bf16[512,8,128]{0,2,1:T(8,128)(2,1)} fusion(f32[8,128,512]{2,1,0:T(8,128)} %fusion.11, bf16[512,8,128]{0,2,1:T(8,128)(2,1)S(1)} %bitcast.89, bf16[8,512,512]{2,1,0:T(8,128)(2,1)} %copy-done.2), kind=kOutput, calls=%fused_computation.16 | convolution fusion | flops 538443776 | bytes 8388608 | tf_op jit(solution)/shard_map/hts,thd->shd/dot_general | solution.py:120
  339.2 1.5 copy.98
  340.7 2.0 pad_maximum_fusion
  (35 shorter events, 0.1 us)
Async XLA Ops:
  6.5 136.7 %all-gather.6.cloned.1.call-start = ((), (), s32[]{:S(2)}) async-start(), calls=%async_computation.1 | async-start | bytes 9437184 | tf_op jit(solution)/shard_map/all_gather | solution.py:61
  7.3 209.7 %all-gather.8.cloned.1.call-start = ((), (), s32[]{:S(2)}) async-start(), calls=%async_computation.3 | async-start | bytes 4718592 | tf_op jit(solution)/shard_map/all_gather | solution.py:19
  7.3 9.8 %copy-start.11 = (bf16[3,512,1024]{2,1,0:T(8,128)(2,1)S(1)}, bf16[3,512,1024]{2,1,0:T(8,128)(2,1)}, u32[]{:S(2)}) copy-start(bf16[3,512,1024]{2,1,0:T(8,128)(2,1)} %param.15) | copy-start | bytes 9437188
  11.5 23.9 %collective-permute-start = (bf16[127,2048]{1,0:T(8,128)(2,1)}, bf16[127,2048]{1,0:T(8,128)(2,1)}, u32[]{:S(2)}, u32[]{:S(2)}) collective-permute-start(bf16[127,2048]{1,0:T(8,128)(2,1)} %slice_bitcast_fusion), channel_id=1, source_target_pairs={{0,1},{1,2},{2,3},{3,4},{4,5},{5,6},{6,7},{8,9},{9,10},{10,11},{11... | collective-permute-start | bytes 1560584 | tf_op jit(solution)/shard_map/ppermute | solution.py:14
  18.9 1.9 copy-start
  19.5 1.3 copy-start.5
  19.5 1.5 copy-start.12
  20.8 214.7 %reduce-scatter.2.cloned.1.call-start = ((), (), s32[]{:S(2)}) async-start(), calls=%async_computation.2 | async-start | bytes 6291456 | tf_op jit(solution)/shard_map/reduce_scatter | solution.py:64
  26.4 10.7 %slice-start = ((bf16[3,512,2048]{2,1,0:T(8,128)(2,1)}), bf16[1,512,2048]{2,1,0:T(8,128)(2,1)S(1)}, s32[]{:S(2)}) async-start(bf16[3,512,2048]{2,1,0:T(8,128)(2,1)} %param.10), calls=%async_computation.5 | async-start | bytes 4194304 | tf_op jit(solution)/shard_map/slice | solution.py:51
  154.7 1.8 copy-start.13
  154.7 1.9 copy-start.14
  154.7 2.0 copy-start.6
  154.8 160.7 %all-gather.10.cloned.1.call-start = ((), (), s32[]{:S(2)}) async-start(), calls=%async_computation.4 | async-start | bytes 4718592 | tf_op jit(solution)/shard_map/all_gather | solution.py:19
  156.6 69.2 %copy-start.3 = (bf16[1,512,1024]{1,2,0:T(8,128)(2,1)}, bf16[1,512,1024]{1,2,0:T(8,128)(2,1)S(1)}, u32[]{:S(2)}) copy-start(bf16[1,512,1024]{1,2,0:T(8,128)(2,1)S(1)} %copy.113) | copy-start | bytes 3145732
  225.7 1.5 copy-start.1
  243.6 1.4 copy-start.7
  245.0 2.5 copy-start.2
  328.9 1.8 copy-start.8
  328.9 2.7 copy-start.9
  331.5 3.0 copy-start.4
  334.5 6.2 %copy-start.10 = (bf16[1,512,1024]{2,1,0:T(8,128)(2,1)S(1)}, bf16[1,512,1024]{2,1,0:T(8,128)(2,1)}, u32[]{:S(2)}) copy-start(bf16[1,512,1024]{2,1,0:T(8,128)(2,1)} %copy.97) | copy-start | bytes 3145732
Sparse Core Ops, SparseCore 0:
  9.5 133.6 all-gather.5
  145.3 71.5 all-gather.7
  219.2 10.2 reduce-scatter.1
  243.3 72.1 all-gather.9
where the time goes:
time: 350 us; the launch traced here: 349 us
  waiting for transfers between devices  169 us (48%)
  matrix products  105 us (30%)
  other arithmetic  30.7 us (9%)
  local copies, waits for them, and re-layouts  24.8 us (7%)
  between operations  13.5 us (4%)
  starting transfers between devices  5.94 us (2%)
    all_gather x2, waiting for transfers between devices, prefix(): pieces = lax.all_gather(value, axis)  118 us
    conv_general_dilated x1, matrix products, depthwise(): lax.conv_general_dilated(extended[None], kernel, (1,), 'VALID', dimension...  65.3 us
    all_gather x1, waiting for transfers between devices, on_device(): shard_rows = lax.all_gather(map_weight, 'ctx', axis=0, tiled=True)  40.9 us
    select_n x14, other arithmetic, turn(): return jnp.where(position < mine, longer, so_far)  17.2 us
    dot_general x1, matrix products, on_device(): jnp.dot(columns, shard_rows, preferred_element_type=jnp.float32)  11.5 us
    ppermute x1, waiting for transfers between devices, from_behind(): lax.ppermute(value, axis, [(source, source + steps) for source in range(l...  8.95 us
  transfers between devices with their start and end apart: 5, of which 4 were waited for; matrix products, arithmetic and copies ran while one was open for 36% of the time, Pallas kernels for 0%

commit v1 on v0

--- a/solution.py
+++ b/solution.py
@@ -6,6 +6,12 @@
 
 DH = 128
 BLK = 512
+
+
+def joined_along(blocks, dim):
+    blocks = jnp.moveaxis(blocks, 0, dim)
+    dims = blocks.shape
+    return blocks.reshape(*dims[:dim], dims[dim] * dims[dim + 1], *dims[dim + 2 :])
 
 
 def from_behind(value, axis, steps):
@@ -58,7 +64,19 @@
     conv_out = depthwise(jnp.concatenate([left_rim, mixed_in], 0), conv_filter)
     teacher_out = (gate_in.astype(jnp.float32) * conv_out).astype(jnp.bfloat16)
     zero_map = jnp.zeros((tok_rows, map_weight.shape[1]), jnp.float32)
-    shard_rows = lax.all_gather(map_weight, "ctx", axis=0, tiled=True)
+    length = lax.axis_size("ctx")
+    pairs = [(i, (i + 1) % length) for i in range(length)]
+    back = [(b, a) for a, b in pairs]
+    lower, upper = ([], [])
+    for step in range(length - 1):
+        if step % 2 == 0:
+            lower.append(lax.ppermute(lower[-1] if lower else map_weight, "ctx", pairs))
+        else:
+            upper.append(lax.ppermute(upper[-1] if upper else map_weight, "ctx", back))
+    blocks = jnp.stack([*lower[::-1], map_weight, *upper])
+    shift = lax.axis_index("ctx") - len(lower)
+    blocks = blocks[(jnp.arange(length) - shift) % length]
+    shard_rows = joined_along(blocks, 0)
     columns = lax.slice_in_dim(teacher_out, 0, shard_rows.shape[0], axis=1)
     partial_map = zero_map + jnp.dot(columns, shard_rows, preferred_element_type=jnp.float32)
     target = lax.psum_scatter(partial_map, "role", scatter_dimension=1, tiled=True)

time: 350 us -> 414 us (1.18)
  starting transfers between devices: 5.94 us -> 33.1 us
  local copies, waits for them, and re-layouts: 24.8 us -> 48.7 us
  waiting for transfers between devices: 169 us -> 179 us
    ppermute x0 -> x7, waiting for transfers between devices: none -> 116 us  [the longest x4 116 us: on_device(): lower.append(lax.ppermute(lower[-1] if lower else map_weight, 'ctx', pairs))]
    all_gather x2, waiting for transfers between devices: 118 us -> 63.3 us  [prefix(): pieces = lax.all_gather(value, axis)]
    all_gather x1 -> x0, waiting for transfers between devices: 40.9 us -> none  [on_device(): shard_rows = lax.all_gather(map_weight, 'ctx', axis=0, tiled=True)]
    ppermute x0 -> x7, starting transfers between devices: none -> 30.4 us  [the longest x3 22.4 us: on_device(): upper.append(lax.ppermute(upper[-1] if upper else map_weight, 'ctx', back))]
    unnamed x32 -> x41, local copies, waits for them, and re-layouts: 4.23 us -> 16 us
    ppermute x1, waiting for transfers between devices: 8.95 us -> 0.01 us  [from_behind(): lax.ppermute(value, axis, [(source, source + steps) for source in range(l...]
    gather x0 -> x1, local copies, waits for them, and re-layouts: none -> 8.22 us  [on_device(): blocks = blocks[(jnp.arange(length) - shift) % length]]
  transfers between devices with their start and end apart: 5 -> 11, of which waited for: 4 -> 4; matrix products, arithmetic and copies ran while one was open for 36% -> 36% of each run, Pallas kernels for 0% -> 0%
where the time goes in v1:
time: 414 us; the launch traced here: 413 us
  waiting for transfers between devices  179 us (43%)
  matrix products  105 us (25%)
  local copies, waits for them, and re-layouts  48.7 us (12%)
  starting transfers between devices  33.1 us (8%)
  other arithmetic  31.8 us (8%)
  between operations  15.2 us (4%)
    ppermute x4, waiting for transfers between devices, on_device(): lower.append(lax.ppermute(lower[-1] if lower else map_weight, 'ctx', pairs))  116 us
    conv_general_dilated x1, matrix products, depthwise(): lax.conv_general_dilated(extended[None], kernel, (1,), 'VALID', dimension...  65.1 us
    all_gather x2, waiting for transfers between devices, prefix(): pieces = lax.all_gather(value, axis)  63.3 us
    ppermute x3, starting transfers between devices, on_device(): upper.append(lax.ppermute(upper[-1] if upper else map_weight, 'ctx', back))  22.4 us
    select_n x14, other arithmetic, turn(): return jnp.where(position < mine, longer, so_far)  17.6 us
    unnamed x41, local copies, waits for them, and re-layouts  16 us
    dot_general x1, matrix products, on_device(): jnp.dot(columns, shard_rows, preferred_element_type=jnp.float32)  11.5 us
  transfers between devices with their start and end apart: 11, of which 4 were waited for; matrix products, arithmetic and copies ran while one was open for 36% of the time, Pallas kernels for 0%

profile of v1, /device:TPU:0, one launch (start us, length us, event | category | flops | bytes accessed | tf_op | source)
XLA Modules:
  0.0 412.9 jit_solution(14903009886015296770)
XLA Ops:
  7.4 2.9 collective-permute-start.1
  10.3 3.0 collective-permute-start.5
  13.3 3.2 fusion.19
  17.7 37.8 %collective-permute-done.1 = bf16[256,2048]{1,0:T(8,128)(2,1)} collective-permute-done((bf16[256,2048]{1,0:T(8,128)(2,1)}, bf16[256,2048]{1,0:T(8,128)(2,1)}, u32[]{:S(2)}, u32[]{:S(2)}) %collective-permute-start.1) | collective-permute-done | bytes 1048608 | tf_op jit(solution)/shard_map/ppermute | solution.py:73
  55.5 2.5 collective-permute-start.2
  58.0 1.2 fusion.20
  59.3 3.0 multiply_convert_fusion
  62.4 0.9 slice_bitcast_fusion
  63.3 2.6 collective-permute-start
  65.9 1.5 rev.7
  67.4 0.9 copy.85
  68.4 26.9 %collective-permute-done.2 = bf16[256,2048]{1,0:T(8,128)(2,1)S(1)} collective-permute-done((bf16[256,2048]{1,0:T(8,128)(2,1)}, bf16[256,2048]{1,0:T(8,128)(2,1)S(1)}, u32[]{:S(2)}, u32[]{:S(2)}) %collective-permute-start.2) | collective-permute-done | bytes 1048608 | tf_op jit(solution)/shard_map/ppermute | solution.py:73
  95.9 3.0 fusion.44
  98.9 0.6 maximum_bitcast_fusion
  99.6 5.2 %collective-permute-start.6 = (bf16[256,2048]{1,0:T(8,128)(2,1)}, bf16[256,2048]{1,0:T(8,128)(2,1)}, u32[]{:S(2)}, u32[]{:S(2)}) collective-permute-start(bf16[256,2048]{1,0:T(8,128)(2,1)} %collective-permute-done.5), channel_id=1, source_target_pairs={{1,0},{2,1},{3,2},{4,3},{5,4},{6,5},{7,6},{0,7},{9,8},{10,9},{11,1... | collective-permute-start | bytes 3145736 | tf_op jit(solution)/shard_map/ppermute | solution.py:75
  104.8 51.2 %collective-permute-done.3 = bf16[256,2048]{1,0:T(8,128)(2,1)} collective-permute-done((bf16[256,2048]{1,0:T(8,128)(2,1)S(1)}, bf16[256,2048]{1,0:T(8,128)(2,1)}, u32[]{:S(2)}, u32[]{:S(2)}) %collective-permute-start.3) | collective-permute-done | bytes 1048608 | tf_op jit(solution)/shard_map/ppermute | solution.py:73
  156.0 2.6 collective-permute-start.4
  158.6 65.1 %fusion = bf16[1,512,2048]{2,0,1:T(2,128)(2,1)} fusion(bf16[128,1,2048]{2,1,0:T(2,128)(2,1)S(1)} %copy.85, bf16[1,639,2048]{2,1,0:T(8,128)(2,1)S(1)} %maximum_bitcast_fusion, bf16[1,512,2048]{2,1,0:T(8,128)(2,1)S(1)} %slice-done), kind=kOutput, calls=%fused_computation.6 | convolution fusion | flops 271581184 | bytes 7335936 | tf_op jit(solution)/shard_map/conv_general_dilated | solution.py:40
  223.7 14.2 %collective-permute-start.7 = (bf16[256,2048]{1,0:T(8,128)(2,1)}, bf16[256,2048]{1,0:T(8,128)(2,1)S(1)}, u32[]{:S(2)}, u32[]{:S(2)}) collective-permute-start(bf16[256,2048]{1,0:T(8,128)(2,1)} %collective-permute-done.6), channel_id=1, source_target_pairs={{1,0},{2,1},{3,2},{4,3},{5,4},{6,5},{7,6},{0,7},{9,8},{10,9},{11,1... | collective-permute-start | bytes 3145736 | tf_op jit(solution)/shard_map/ppermute | solution.py:75
  237.9 2.4 bitcast_dynamic-update-slice_fusion.7
  240.2 2.3 bitcast_dynamic-update-slice_fusion.6
  242.6 1.1 bitcast_dynamic-update-slice_fusion.5
  243.6 2.3 bitcast_dynamic-update-slice_fusion.4
  246.0 1.1 bitcast_dynamic-update-slice_fusion.3
  247.1 2.3 bitcast_dynamic-update-slice_fusion.2
  249.4 2.3 bitcast_dynamic-update-slice_fusion.1
  251.7 1.1 bitcast_dynamic-update-slice_fusion
  252.8 8.2 %gather_fusion = bf16[8,256,2048]{2,1,0:T(8,128)(2,1)} fusion(bf16[8,256,2048]{2,1,0:T(8,128)(2,1)} %bitcast_dynamic-update-slice_fusion, s32[1024]{0:T(1024)} %pad_clamp_fusion), kind=kCustom, calls=%fused_computation | custom fusion | bytes 16777248 | tf_op jit(solution)/shard_map/gather | solution.py:78
  261.0 11.5 %fusion.2 = f32[512,2048]{1,0:T(8,128)} fusion(bf16[2048,2048]{1,0:T(8,128)(2,1)} %bitcast.113, bf16[1,512,2048]{2,0,1:T(2,128)(2,1)} %fusion), kind=kOutput, calls=%fused_computation.12 | convolution fusion | flops 4294967296 | bytes 14680064 | tf_op jit(solution)/shard_map/dot_general | solution.py:81
  272.6 1.6 copy.113
  274.4 3.3 select_convert_fusion.1
  277.8 9.1 %while.28 = (s32[]{:T(128)}, f32[8,128,128]{2,1,0:T(8,128)S(1)}, s32[]{:T(128)}, f32[8,8,128,128]{3,2,1,0:T(8,128)}, s32[]{:T(128)}, /*index=5*/s32[]{:T(128)}) while((s32[]{:T(128)}, f32[8,128,128]{2,1,0:T(8,128)S(1)}, s32[]{:T(128)}, f32[8,8,128,128]{3,2,1,0:T(8,128)}, s32[]{:T(128)}, /*index=5*/s32[]{:T(128)}) %tuple.73), condition=%wide.region_1.2_spmd.clone, body=%wide.region_0.1_spmd.clone.sunk | while | flops 393220 | bytes 1572957 | solution.py:35
  277.8 1.3 add_select_fusion.4
  279.1 1.3 add_select_fusion.4
  280.4 1.2 add_select_fusion.4
  281.6 1.4 add_select_fusion.4
  283.0 1.2 add_select_fusion.4
  284.3 1.3 add_select_fusion.4
  285.6 1.2 add_select_fusion.4
  287.3 5.0 %fusion.9 = f32[512,8,128]{0,2,1:T(8,128)} fusion(f32[8,128,512]{2,1,0:T(8,128)S(1)} %fusion.15, bf16[8,512,512]{2,1,0:T(8,128)(2,1)} %select_convert_fusion.1, bf16[512,8,128]{0,2,1:T(8,128)(2,1)S(1)} %bitcast.98), kind=kOutput, calls=%fused_computation.22 | convolution fusion | flops 537919488 | bytes 9437184 | tf_op jit(solution)/shard_map/hts,she->the/dot_general | solution.py:104
  292.3 3.0 copy.86
  295.3 3.5 multiply_convert_fusion.2
  298.8 1.5 copy.114
  300.3 1.6 convolution_bitcast_fusion
  302.0 1.0 copy.92
  303.5 1.4 select_convert_fusion
  304.8 2.5 fusion.8
  307.3 2.3 copy.97
  309.6 4.4 %fusion.21 = f32[8,128,512]{2,1,0:T(8,128)} fusion(bf16[512,8,128]{0,2,1:T(8,128)(2,1)S(1)} %bitcast.104, bf16[8,512,512]{2,1,0:T(8,128)(2,1)} %select_convert_fusion.1), kind=kOutput, calls=%fused_computation.54 | convolution fusion | flops 536870912 | bytes 7340032 | tf_op jit(solution)/shard_map/hts,the->she/dot_general | solution.py:142
  314.0 63.3 %all-gather.7.cloned.1.call-done = f32[64,128,128]{2,1,0:T(8,128)} async-done(((f32[8,128,128]{2,1,0:T(8,128)}), f32[64,128,128]{2,1,0:T(8,128)}) %all-gather.7.cloned.1.call-update) | async-done | bytes 4194320 | tf_op jit(solution)/shard_map/all_gather | solution.py:25
  377.3 4.6 %rev.8 = f32[8,8,128,128]{3,2,1,0:T(8,128)} reverse(f32[8,8,128,128]{3,2,1,0:T(8,128)} %bitcast.115), dimensions={0} | reverse | bytes 8388608 | tf_op jit(solution)/shard_map/rev | solution.py:27
  382.0 8.8 %while.29 = (s32[]{:T(128)}, f32[8,128,128]{2,1,0:T(8,128)S(1)}, s32[]{:T(128)}, f32[8,8,128,128]{3,2,1,0:T(8,128)}, s32[]{:T(128)}, /*index=5*/s32[]{:T(128)}) while((s32[]{:T(128)}, f32[8,128,128]{2,1,0:T(8,128)S(1)}, s32[]{:T(128)}, f32[8,8,128,128]{3,2,1,0:T(8,128)}, s32[]{:T(128)}, /*index=5*/s32[]{:T(128)}) %tuple.64), condition=%wide.region_5.6_spmd.clone, body=%wide.region_4.5_spmd.clone.sunk | while | flops 393220 | bytes 1572957 | solution.py:35
  382.0 1.3 add_select_fusion.5
  383.3 1.2 add_select_fusion.5
  384.6 1.2 add_select_fusion.5
  385.8 1.2 add_select_fusion.5
  387.1 1.2 add_select_fusion.5
  388.3 1.2 add_select_fusion.5
  389.6 1.2 add_select_fusion.5
  391.2 4.1 fusion.6
  395.3 2.4 copy.98
  397.7 3.1 multiply_convert_fusion.1
  400.7 1.5 copy.99
  402.2 3.2 pad_maximum_fusion
  (59 shorter events, 3.4 us)
Async XLA Ops:
  7.4 270.4 %all-gather.5.cloned.1.call-start = ((), (), s32[]{:S(2)}) async-start(), calls=%async_computation.2 | async-start | bytes 4718592 | tf_op jit(solution)/shard_map/all_gather | solution.py:25
  7.4 48.1 %collective-permute-start.1 = (bf16[256,2048]{1,0:T(8,128)(2,1)}, bf16[256,2048]{1,0:T(8,128)(2,1)}, u32[]{:S(2)}, u32[]{:S(2)}) collective-permute-start(bf16[256,2048]{1,0:T(8,128)(2,1)} %param.12), channel_id=1, source_target_pairs={{0,1},{1,2},{2,3},{3,4},{4,5},{5,6},{6,7},{7,0},{8,9},{9,10},{10,1... | collective-permute-start | bytes 3145736 | tf_op jit(solution)/shard_map/ppermute | solution.py:73
  10.3 89.3 %collective-permute-start.5 = (bf16[256,2048]{1,0:T(8,128)(2,1)}, bf16[256,2048]{1,0:T(8,128)(2,1)}, u32[]{:S(2)}, u32[]{:S(2)}) collective-permute-start(bf16[256,2048]{1,0:T(8,128)(2,1)} %param.12), channel_id=1, source_target_pairs={{1,0},{2,1},{3,2},{4,3},{5,4},{6,5},{7,6},{0,7},{9,8},{10,9},{11,1... | collective-permute-start | bytes 3145736 | tf_op jit(solution)/shard_map/ppermute | solution.py:75
  17.1 45.2 %copy-start.5 = (bf16[1,512,1024]{1,2,0:T(8,128)(2,1)}, bf16[1,512,1024]{1,2,0:T(8,128)(2,1)S(1)}, u32[]{:S(2)}) copy-start(bf16[1,512,1024]{1,2,0:T(8,128)(2,1)S(1)} %copy.75) | copy-start | bytes 3145732
  17.7 44.7 %copy-start = (bf16[1,512,1024]{1,2,0:T(8,128)(2,1)}, bf16[1,512,1024]{1,2,0:T(8,128)(2,1)S(1)}, u32[]{:S(2)}) copy-start(bf16[1,512,1024]{1,2,0:T(8,128)(2,1)S(1)} %copy.112) | copy-start | bytes 3145732
  55.5 39.7 %collective-permute-start.2 = (bf16[256,2048]{1,0:T(8,128)(2,1)}, bf16[256,2048]{1,0:T(8,128)(2,1)S(1)}, u32[]{:S(2)}, u32[]{:S(2)}) collective-permute-start(bf16[256,2048]{1,0:T(8,128)(2,1)} %collective-permute-done.1), channel_id=1, source_target_pairs={{0,1},{1,2},{2,3},{3,4},{4,5},{5,6},{6,7},{7,0},{8,9},{9,10},{10,1... | collective-permute-start | bytes 3145736 | tf_op jit(solution)/shard_map/ppermute | solution.py:73
  59.3 236.1 %reduce-scatter.2.cloned.1.call-start = ((), (), s32[]{:S(2)}) async-start(), calls=%async_computation.1 | async-start | bytes 6291456 | tf_op jit(solution)/shard_map/reduce_scatter | solution.py:82
  63.3 2.6 copy-start.13
  63.3 35.6 %collective-permute-start = (bf16[127,2048]{1,0:T(8,128)(2,1)}, bf16[127,2048]{1,0:T(8,128)(2,1)S(1)}, u32[]{:S(2)}, u32[]{:S(2)}) collective-permute-start(bf16[127,2048]{1,0:T(8,128)(2,1)} %slice_bitcast_fusion), channel_id=1, source_target_pairs={{0,1},{1,2},{2,3},{3,4},{4,5},{5,6},{6,7},{8,9},{9,10},{10,11},{11... | collective-permute-start | bytes 1560584 | tf_op jit(solution)/shard_map/ppermute | solution.py:20
  95.2 4.3 %copy-start.11 = (bf16[256,2048]{1,0:T(8,128)(2,1)}, bf16[256,2048]{1,0:T(8,128)(2,1)S(1)}, u32[]{:S(2)}) copy-start(bf16[256,2048]{1,0:T(8,128)(2,1)S(1)} %collective-permute-done.2) | copy-start | bytes 3145732
  95.2 60.7 %collective-permute-start.3 = (bf16[256,2048]{1,0:T(8,128)(2,1)S(1)}, bf16[256,2048]{1,0:T(8,128)(2,1)}, u32[]{:S(2)}, u32[]{:S(2)}) collective-permute-start(bf16[256,2048]{1,0:T(8,128)(2,1)S(1)} %collective-permute-done.2), channel_id=1, source_target_pairs={{0,1},{1,2},{2,3},{3,4},{4,5},{5,6},{6,7},{7,0},{8,9},{9,10},{10,1... | collective-permute-start | bytes 3145736 | tf_op jit(solution)/shard_map/ppermute | solution.py:73
  98.9 59.7 %slice-start = ((bf16[3,512,2048]{2,1,0:T(8,128)(2,1)}), bf16[1,512,2048]{2,1,0:T(8,128)(2,1)S(1)}, s32[]{:S(2)}) async-start(bf16[3,512,2048]{2,1,0:T(8,128)(2,1)} %param.10), calls=%async_computation.4 | async-start | bytes 4194304 | tf_op jit(solution)/shard_map/slice | solution.py:57
  99.6 124.1 %collective-permute-start.6 = (bf16[256,2048]{1,0:T(8,128)(2,1)}, bf16[256,2048]{1,0:T(8,128)(2,1)}, u32[]{:S(2)}, u32[]{:S(2)}) collective-permute-start(bf16[256,2048]{1,0:T(8,128)(2,1)} %collective-permute-done.5), channel_id=1, source_target_pairs={{1,0},{2,1},{3,2},{4,3},{5,4},{6,5},{7,6},{0,7},{9,8},{10,9},{11,1... | collective-permute-start | bytes 3145736 | tf_op jit(solution)/shard_map/ppermute | solution.py:75
  156.0 81.9 %collective-permute-start.4 = (bf16[256,2048]{1,0:T(8,128)(2,1)}, bf16[256,2048]{1,0:T(8,128)(2,1)}, u32[]{:S(2)}, u32[]{:S(2)}) collective-permute-start(bf16[256,2048]{1,0:T(8,128)(2,1)} %collective-permute-done.3), channel_id=1, source_target_pairs={{0,1},{1,2},{2,3},{3,4},{4,5},{5,6},{6,7},{7,0},{8,9},{9,10},{10,1... | collective-permute-start | bytes 3145736 | tf_op jit(solution)/shard_map/ppermute | solution.py:73
  223.7 18.9 %copy-start.12 = (bf16[256,2048]{1,0:T(8,128)(2,1)S(1)}, bf16[256,2048]{1,0:T(8,128)(2,1)}, u32[]{:S(2)}) copy-start(bf16[256,2048]{1,0:T(8,128)(2,1)} %copy-done.11) | copy-start | bytes 3145732
  223.7 22.3 %copy-start.10 = (bf16[256,2048]{1,0:T(8,128)(2,1)S(1)}, bf16[256,2048]{1,0:T(8,128)(2,1)}, u32[]{:S(2)}) copy-start(bf16[256,2048]{1,0:T(8,128)(2,1)} %param.12) | copy-start | bytes 3145732
  223.7 28.0 %collective-permute-start.7 = (bf16[256,2048]{1,0:T(8,128)(2,1)}, bf16[256,2048]{1,0:T(8,128)(2,1)S(1)}, u32[]{:S(2)}, u32[]{:S(2)}) collective-permute-start(bf16[256,2048]{1,0:T(8,128)(2,1)} %collective-permute-done.6), channel_id=1, source_target_pairs={{1,0},{2,1},{3,2},{4,3},{5,4},{6,5},{7,6},{0,7},{9,8},{10,9},{11,1... | collective-permute-start | bytes 3145736 | tf_op jit(solution)/shard_map/ppermute | solution.py:75
  272.5 1.7 copy-start.14
  272.5 1.7 copy-start.15
  272.5 1.9 copy-start.6
  272.6 104.8 %all-gather.7.cloned.1.call-start = ((), (), s32[]{:S(2)}) async-start(), calls=%async_computation.3 | async-start | bytes 4718592 | tf_op jit(solution)/shard_map/all_gather | solution.py:25
  274.2 12.6 %copy-start.3 = (bf16[1,512,1024]{1,2,0:T(8,128)(2,1)}, bf16[1,512,1024]{1,2,0:T(8,128)(2,1)S(1)}, u32[]{:S(2)}) copy-start(bf16[1,512,1024]{1,2,0:T(8,128)(2,1)S(1)} %copy.113) | copy-start | bytes 3145732
  277.7 9.6 %copy-start.1 = (bf16[1,512,1024]{1,2,0:T(8,128)(2,1)S(1)}, bf16[1,512,1024]{1,2,0:T(8,128)(2,1)}, u32[]{:S(2)}) copy-start(bf16[1,512,1024]{1,2,0:T(8,128)(2,1)} %copy-done) | copy-start | bytes 3145732
  303.4 1.4 copy-start.7
  304.8 2.5 copy-start.2
  382.0 9.3 %copy-start.4 = (bf16[1,512,1024]{1,2,0:T(8,128)(2,1)S(1)}, bf16[1,512,1024]{1,2,0:T(8,128)(2,1)}, u32[]{:S(2)}) copy-start(bf16[1,512,1024]{1,2,0:T(8,128)(2,1)} %copy-done.3) | copy-start | bytes 3145732
  391.2 6.4 %copy-start.8 = (bf16[1,512,1024]{1,2,0:T(8,128)(2,1)S(1)}, bf16[1,512,1024]{1,2,0:T(8,128)(2,1)}, u32[]{:S(2)}) copy-start(bf16[1,512,1024]{1,2,0:T(8,128)(2,1)} %copy-done.5) | copy-start | bytes 3145732
  395.3 6.9 %copy-start.9 = (bf16[1,512,1024]{2,1,0:T(8,128)(2,1)S(1)}, bf16[1,512,1024]{2,1,0:T(8,128)(2,1)}, u32[]{:S(2)}) copy-start(bf16[1,512,1024]{2,1,0:T(8,128)(2,1)} %copy.97) | copy-start | bytes 3145732
Sparse Core Ops, SparseCore 0:
  59.4 153.7 all-gather.4
  303.1 74.1 all-gather.6
Sparse Core Ops, SparseCore 1:
  272.6 12.6 reduce-scatter.1
